TPU v7x, 128 devices: a whole 4x4x4 slice. The times are simulated.
128 devices in a mesh: fsdp: 16 (over y_lo, z, core), tp: 8 (over x, y_hi).
Axes of the slice: x: 4, y: 4 (y_hi: 2, y_lo: 2; y = y_hi * 2 + y_lo), z: 4, core: 2. Of those that a mesh axis runs over, the one named last changes fastest.
Arguments:
- hidden_in: bfloat16 [1024, 4096], P('fsdp'), may hold values from -3 to 3
- queries: bfloat16 [2, 1024, 8192], P(None, ('fsdp', 'tp')), may hold values from -170 to 170
- key_cache: bfloat16 [1024, 256, 512], P(('fsdp', 'tp')), may hold values from -6 to 6
- value_cache: bfloat16 [1024, 256, 512], P(('fsdp', 'tp')), may hold values from -6 to 6
- new_keys: bfloat16 [2, 1024, 512], P(None, ('fsdp', 'tp')), may hold values from -6 to 6
- new_values: bfloat16 [2, 1024, 512], P(None, ('fsdp', 'tp')), may hold values from -6 to 6
- lengths: int32 [1024], P(('fsdp', 'tp')), may hold values from 2 to 256
- routes: int32 [2, 1024, 8], P(None, 'fsdp'), may hold values from 0 to 127, all different within a row; in each aligned block of 64 rows (0 to 63, 64 to 127, ..., all dimensions but the last counted through in order) at most 8 rows name the same one
- route_weights: float32 [2, 1024, 8], P(None, 'fsdp'), may hold values from 0.05 to 1
- norm_gain: float32 [4096], replicated, may hold values from 0.1 to 1.9
- gate_master: float32 [8, 1536, 4096], P(None, ('fsdp', 'tp')), may hold values from -0.09375 to 0.09375
- up_master: float32 [8, 1536, 4096], P(None, ('fsdp', 'tp')), may hold values from -0.09375 to 0.09375
- down_master: float32 [8, 1536, 4096], P(None, ('fsdp', 'tp')), may hold values from -0.3125 to 0.3125
- out_proj: bfloat16 [8192, 4096], P('tp'), may hold values from -0.0625 to 0.0625
Outputs:
- hidden_out: bfloat16 [1024, 4096], P('fsdp', 'tp')
- scale_log2: float32 [3, 8, 12, 32], replicated
Inputs may be any that keep to these rules, and one draw needn't show every extreme that they name: `routes`: within one step and one index of fsdp (aligned blocks of 64 rows), no expert is named by more than 8 rows.
All inputs are finite; a program needn't handle non-finite values.
Results may differ from a plain program's by a relative error of at most 0.0095.
Values may be sent and summed in bfloat16 or wider, within the bound.
A program may use at most 256 MiB of HBM per device.

v0:
```python
import jax
import jax.numpy as jnp
from jax import lax
from jax.sharding import PartitionSpec as P

D = 4096
FF = 1536
QH = 64
KVH = 4
HD = 128
BLOCK = 128
WIN = 8
CAP = 8
neg_fill = -1e30
epsilon = 1e-06
fp_limit = 448.0
grid_floor = 2.0 ** (-10)
least_exponent = -6.0


def cut_along(array, dim, peers):
    before, after = (array.shape[:dim], array.shape[dim + 1 :])
    return jnp.moveaxis(array.reshape(*before, peers, -1, *after), dim, 0)


def sent_and_summed(array, axis, dim):
    blocks = cut_along(array, dim, lax.axis_size(axis))
    arrived = lax.all_to_all(blocks, axis, split_axis=0, concat_axis=0, tiled=True)
    return arrived.astype(jnp.float32).sum(axis=0)


def copy_for_each(array, axis):
    peers = lax.axis_size(axis)
    return lax.all_to_all(
        jnp.broadcast_to(array[None], (peers, *array.shape)), axis, 0, 0, tiled=True
    )


def joined_along(blocks, dim):
    blocks = jnp.moveaxis(blocks, 0, dim)
    lengths = blocks.shape
    return blocks.reshape(*lengths[:dim], lengths[dim] * lengths[dim + 1], *lengths[dim + 2 :])


def collect(array, axis, dim):
    blocks = copy_for_each(array, axis)
    return joined_along(blocks, dim)


def grid_round(values):
    magnitude = jnp.abs(values)
    exponent = jnp.maximum(jnp.floor(jnp.log2(jnp.maximum(magnitude, grid_floor))), least_exponent)
    spacing = jnp.exp2(exponent - 3.0)
    return jnp.sign(values) * jnp.floor(magnitude / spacing + 0.5) * spacing


def row_scales(scales, owner_map):
    return jnp.einsum(
        "sb,xwbc->xwsc", owner_map.astype(jnp.float32), scales, precision=lax.Precision.HIGHEST
    )


def owner_blocks(owner_rows):
    return (owner_rows // BLOCK)[:, None] == jnp.arange(FF // BLOCK, dtype=jnp.int32)[None, :]


def dequantize(shard_piece, shard_rows, tp_count, tp_pos, scales):
    count = shard_piece.shape[2]
    gathered_index = jnp.arange(count, dtype=jnp.int32)
    owner_rows = (
        gathered_index // shard_rows * tp_count + tp_pos
    ) * shard_rows + gathered_index % shard_rows
    factors = row_scales(scales, owner_blocks(owner_rows))
    tiles = shard_piece.astype(jnp.float32).reshape(3, WIN, count, D // BLOCK, BLOCK)
    return (tiles * factors[..., None]).astype(jnp.bfloat16).reshape(3, WIN, count, D)


def attention_rows(queries_now, cache_keys, cache_values, fresh_keys, fresh_values, lengths):
    row_count = queries_now.shape[0]
    positions = cache_keys.shape[1]
    group = QH // KVH
    score_scale = HD ** (-0.5)
    fresh_count = fresh_keys.shape[0]
    query_heads = queries_now.reshape(row_count, KVH, group, HD)
    key_heads = cache_keys.reshape(row_count, positions, KVH, HD)
    value_heads = cache_values.reshape(row_count, positions, KVH, HD)
    fresh_key_heads = fresh_keys.reshape(fresh_count, row_count, KVH, HD)
    fresh_value_heads = fresh_values.reshape(fresh_count, row_count, KVH, HD)
    cached_scores = (
        jnp.einsum("rkgd,rpkd->rkgp", query_heads, key_heads, preferred_element_type=jnp.float32)
        * score_scale
    )
    fresh_scores = (
        jnp.einsum(
            "rkgd,srkd->rkgs", query_heads, fresh_key_heads, preferred_element_type=jnp.float32
        )
        * score_scale
    )
    alive_mask = (jnp.arange(positions, dtype=jnp.int32)[None, :] < lengths[:, None])[
        :, None, None, :
    ]
    peak_score = jnp.maximum(
        jnp.max(jnp.where(alive_mask, cached_scores, neg_fill), axis=-1),
        jnp.max(fresh_scores, axis=-1),
    )
    cached_weights = jnp.where(alive_mask, jnp.exp(cached_scores - peak_score[..., None]), 0.0)
    fresh_weights = jnp.exp(fresh_scores - peak_score[..., None])
    weight_sum = jnp.sum(cached_weights, axis=-1) + jnp.sum(fresh_weights, axis=-1)
    cached_probs = (cached_weights / weight_sum[..., None]).astype(jnp.bfloat16)
    fresh_probs = (fresh_weights / weight_sum[..., None]).astype(jnp.bfloat16)
    output = jnp.einsum(
        "rkgp,rpkd->rkgd", cached_probs, value_heads, preferred_element_type=jnp.float32
    )
    output = output + jnp.einsum(
        "rkgs,srkd->rkgd", fresh_probs, fresh_value_heads, preferred_element_type=jnp.float32
    )
    return output.astype(jnp.bfloat16).reshape(row_count, QH * HD)


def routing_tables(routes, route_weights, capacity):
    weight_sum = jnp.sum(route_weights, axis=1)
    experts = jnp.arange(WIN, dtype=jnp.int32)
    matches = routes[None, :, :] == experts[:, None, None]
    chosen = jnp.any(matches, axis=2)
    gate_share = (
        jnp.sum(jnp.where(matches, route_weights[None, :, :], 0.0), axis=2) / weight_sum[None, :]
    )
    slot_index = jnp.cumsum(chosen.astype(jnp.int32), axis=1) - 1
    places = jnp.arange(capacity, dtype=jnp.int32)
    picked = (slot_index[:, None, :] == places[None, :, None]) & chosen[:, None, :]
    return (picked.astype(jnp.bfloat16), picked.astype(jnp.float32) * gate_share[:, None, :])


def expert_rows(selected, gate_rows, up_rows, down_rows):
    gate_act = jnp.einsum("ecd,ehd->ech", selected, gate_rows, preferred_element_type=jnp.float32)
    up_act = jnp.einsum("ecd,ehd->ech", selected, up_rows, preferred_element_type=jnp.float32)
    product = (jax.nn.silu(gate_act) * up_act).astype(jnp.bfloat16)
    return jnp.einsum("ech,ehd->ecd", product, down_rows, preferred_element_type=jnp.float32)


def local_experts(selected, weighted, restored):
    outputs = expert_rows(selected, restored[0], restored[1], restored[2])
    return jnp.einsum("ecr,ecd->rd", weighted, outputs, precision=lax.Precision.HIGHEST)


def local(
    hidden_in,
    queries,
    key_cache,
    value_cache,
    new_keys,
    new_values,
    lengths,
    routes,
    route_weights,
    norm_gain,
    gate_master,
    up_master,
    down_master,
    out_proj,
):
    tp_count = lax.axis_size("tp")
    fsdp_pos = lax.axis_index("fsdp")
    tp_pos = lax.axis_index("tp")
    shard_rows = gate_master.shape[1]
    masters = jnp.stack([gate_master, up_master, down_master])
    owned_rows = (fsdp_pos * tp_count + tp_pos) * shard_rows + jnp.arange(
        shard_rows, dtype=jnp.int32
    )
    owner_map = owner_blocks(owned_rows)
    magnitude = jnp.max(jnp.abs(masters).reshape(3, WIN, shard_rows, D // BLOCK, BLOCK), axis=4)
    partial_max = jnp.max(
        jnp.where(owner_map[None, None, :, :, None], magnitude[:, :, :, None, :], 0.0), axis=2
    )
    block_max = lax.pmax(partial_max, ("fsdp", "tp"))
    scales = (block_max + epsilon) / fp_limit
    scale_log2 = jnp.log2(scales)
    local_factors = row_scales(scales, owner_map)
    tiles = masters.reshape(3, WIN, shard_rows, D // BLOCK, BLOCK)
    quantized = (
        grid_round(tiles / local_factors[..., None])
        .astype(jnp.bfloat16)
        .reshape(3, WIN, shard_rows, D)
    )
    gathered = lax.all_gather(quantized, "fsdp", axis=2, tiled=True)
    restored = dequantize(gathered, shard_rows, tp_count, tp_pos, scales)
    share_cols = D // tp_count
    own_start = tp_pos * share_cols
    current = lax.dynamic_slice_in_dim(hidden_in, own_start, share_cols, 1)
    for step_index in range(2):
        heads_local = attention_rows(
            queries[step_index],
            key_cache,
            value_cache,
            new_keys[: step_index + 1],
            new_values[: step_index + 1],
            lengths,
        )
        regrouped = lax.all_to_all(heads_local, "tp", split_axis=1, concat_axis=0, tiled=True)
        projected = jnp.dot(regrouped, out_proj, preferred_element_type=jnp.float32)
        mixed = (
            current.astype(jnp.float32) + sent_and_summed(projected.astype(jnp.bfloat16), "tp", 1)
        ).astype(jnp.bfloat16)
        values = mixed.astype(jnp.float32)
        squares = lax.psum(jnp.sum(values * values, axis=1), "tp")
        inverse = lax.rsqrt(squares / D + epsilon)
        own_gain = lax.dynamic_slice_in_dim(norm_gain, own_start, share_cols, 0)
        normed_share = (values * inverse[:, None] * own_gain[None, :]).astype(jnp.bfloat16)
        normed = collect(normed_share, "tp", 1)
        picked, weighted = routing_tables(routes[step_index], route_weights[step_index], CAP)
        selected = jnp.einsum(
            "ecr,rd->ecd", picked, normed, preferred_element_type=jnp.float32
        ).astype(jnp.bfloat16)
        partial_value = local_experts(selected, weighted, restored)
        current = (
            mixed.astype(jnp.float32) + sent_and_summed(partial_value.astype(jnp.bfloat16), "tp", 1)
        ).astype(jnp.bfloat16)
    return (current, scale_log2)


def solution(mesh):
    in_specs = (
        P("fsdp", None),
        P(None, ("fsdp", "tp"), None),
        P(("fsdp", "tp"), None, None),
        P(("fsdp", "tp"), None, None),
        P(None, ("fsdp", "tp"), None),
        P(None, ("fsdp", "tp"), None),
        P(("fsdp", "tp")),
        P(None, "fsdp", None),
        P(None, "fsdp", None),
        P(),
        P(None, ("fsdp", "tp"), None),
        P(None, ("fsdp", "tp"), None),
        P(None, ("fsdp", "tp"), None),
        P("tp", None),
    )
    out_specs = (P("fsdp", "tp"), P())
    return jax.shard_map(local, mesh=mesh, in_specs=in_specs, out_specs=out_specs, check_vma=False)
```

profile of v0, /device:TPU:0, one launch (start us, length us, event | category | flops | bytes accessed | tf_op | source)
XLA Modules:
  0.0 576.3 jit_solution(13156694128293218370)
XLA Ops:
  11.7 69.4 %pmax.7 = f32[3,8,12,32]{3,2,1,0:T(8,128)S(1)} all-reduce(f32[3,8,12,32]{3,2,1,0:T(8,128)S(1)} %copy.88), channel_id=1, replica_groups=mesh['fsdp'=16,'tp'=8] {'fsdp','tp'}, use_global_device_ids=true, to_apply=%region_11.12 | all-reduce | flops 9216 | bytes 73728 | tf_op jit(solution)/shard_map/pmax | solution.py:175
  81.6 7.7 %multiply_convert_fusion = bf16[3,8,12,4096]{3,1,2,0:T(8,128)(2,1)} fusion(f32[1,8,12,4096]{3,1,2,0:T(8,128)} %bitcast.173, f32[1,8,12,4096]{3,1,2,0:T(8,128)} %bitcast.175, f32[1,8,12,4096]{3,1,2,0:T(8,128)} %bitcast.177, f32[3,8,12,32]{1,3,2,0:T(8,128)S(1)} %copy.89), kind=kLoop, calls=%fused_computation.6 | loop fusion | flops 20054016 | bytes 7114752 | tf_op jit(solution)/shard_map/convert_element_type | solution.py:182
  100.4 4.2 all-to-all-done
  104.6 5.2 convolution_convert_fusion.3
  117.9 7.5 %all-to-all-done.1 = bf16[8,64,512]{2,1,0:T(8,128)(2,1)S(1)} async-done(((bf16[8,64,512]{2,1,0:T(8,128)(2,1)}), bf16[8,64,512]{2,1,0:T(8,128)(2,1)S(1)}, u32[]{:S(2)}, u32[]{:S(2)}) %all-to-all-start.1) | async-done | bytes 524320 | tf_op jit(solution)/shard_map/all_to_all | solution.py:28
  129.9 24.9 %psum.14 = f32[64]{0:T(128)S(1)} all-reduce(f32[64]{0:T(128)S(1)} %get-tuple-element.16), channel_id=1, replica_groups=mesh['fsdp'=16,'tp'=8] {'tp'}, use_global_device_ids=true, to_apply=%region_8.9 | all-reduce | flops 64 | bytes 512 | tf_op jit(solution)/shard_map/psum | solution.py:205
  159.3 5.0 convolution_convert_fusion.1
  169.0 3.9 all-to-all-start.5
  173.8 122.2 %all-gather.2.cloned.1.call-done = bf16[3,8,192,4096]{3,1,2,0:T(8,128)(2,1)} async-done(((bf16[3,8,12,4096]{3,1,2,0:T(8,128)(2,1)}), bf16[3,8,192,4096]{3,1,2,0:T(8,128)(2,1)}) %all-gather.2.cloned.1.call-update) | async-done | bytes 37748752 | tf_op jit(solution)/shard_map/all_gather | solution.py:185
  296.0 36.6 %bitcast_convert_fusion = f32[3,8,192,32,128]{4,1,3,2,0:T(8,128)} fusion(bf16[3,8,192,4096]{3,1,2,0:T(8,128)(2,1)} %all-gather.2.cloned.1.call-done), kind=kLoop, calls=%fused_computation.2 | loop fusion | flops 18874368 | bytes 113246208 | tf_op jit(solution)/shard_map/reshape | solution.py:74
  332.7 38.8 %fusion = bf16[3,8,192,32,128]{4,3,2,1,0:T(8,128)(2,1)} fusion(f32[3,8,192,32,128]{4,1,3,2,0:T(8,128)} %bitcast_convert_fusion, f32[3,8,192,32]{3,2,1,0:T(8,128)} %copy.90), kind=kLoop, calls=%fused_computation.1 | loop fusion | flops 37748736 | bytes 113836032 | tf_op jit(solution)/shard_map/convert_element_type | solution.py:75
  371.5 25.3 %fusion.120 = (bf16[1,8,192,32,128]{4,3,2,1,0:T(8,128)(2,1)}, bf16[1,8,192,32,128]{4,3,2,1,0:T(8,128)(2,1)}, bf16[1,8,192,32,128]{4,3,2,1,0:T(8,128)(2,1)}) fusion(bf16[3,8,192,32,128]{4,3,2,1,0:T(8,128)(2,1)} %fusion), kind=kLoop, calls=%fused_computation.189 | loop fusion | bytes 75497472 | tf_op jit(solution)/shard_map/slice | solution.py:142
  396.8 19.3 %squeeze.16 = bf16[8,192,4096]{2,1,0:T(8,128)(2,1)} reshape(bf16[1,8,192,32,128]{4,3,2,1,0:T(8,128)(2,1)} %get-tuple-element.19) | data formatting | bytes 25165824 | tf_op jit(solution)/shard_map/squeeze | solution.py:142
  416.1 19.3 %squeeze.7 = bf16[8,192,4096]{2,1,0:T(8,128)(2,1)} reshape(bf16[1,8,192,32,128]{4,3,2,1,0:T(8,128)(2,1)} %get-tuple-element.20) | data formatting | bytes 25165824 | tf_op jit(solution)/shard_map/squeeze | solution.py:142
  435.4 19.3 %squeeze.6 = bf16[8,192,4096]{2,1,0:T(8,128)(2,1)} reshape(bf16[1,8,192,32,128]{4,3,2,1,0:T(8,128)(2,1)} %get-tuple-element.18) | data formatting | bytes 25165824 | tf_op jit(solution)/shard_map/squeeze | solution.py:142
  454.7 7.9 %fusion.122 = f32[8,8,192]{2,1,0:T(8,128)S(1)} fusion(bf16[8,8,4096]{2,1,0:T(8,128)(2,1)S(1)} %convolution_convert_fusion.2, bf16[8,192,4096]{2,1,0:T(8,128)(2,1)} %squeeze.6), kind=kOutput, calls=%fused_computation.191 | convolution fusion | flops 100663296 | bytes 13156352 | tf_op jit(solution)/shard_map/ecd,ehd->ech/dot_general | solution.py:135
  462.6 10.7 %fusion.39 = f32[8,8,4096]{2,1,0:T(8,128)S(1)} fusion(bf16[8,192,4096]{2,1,0:T(8,128)(2,1)} %squeeze.16, bf16[8,8,4096]{2,1,0:T(8,128)(2,1)S(1)} %convolution_convert_fusion.2, bf16[8,192,4096]{2,1,0:T(8,128)(2,1)} %squeeze.7, f32[8,8,192]{2,1,0:T(8,128)S(1)} %fusion.122), kind=kOutput, calls=%fused_computation.48 | convolution fusion | flops 201400320 | bytes 26787840 | tf_op jit(solution)/shard_map/ech,ehd->ecd/dot_general | solution.py:138
  475.8 6.4 %all-to-all-start.3 = ((bf16[8,64,512]{2,1,0:T(8,128)(2,1)}), bf16[8,64,512]{2,1,0:T(8,128)(2,1)S(1)}, u32[]{:S(2)}, u32[]{:S(2)}) async-start(bf16[8,64,512]{2,1,0:T(8,128)(2,1)} %bitcast.169), calls=%async_computation.3 | async-start | bytes 1048576 | tf_op jit(solution)/shard_map/all_to_all | solution.py:28
  482.5 11.0 %all-to-all-done.3 = bf16[8,64,512]{2,1,0:T(8,128)(2,1)S(1)} async-done(((bf16[8,64,512]{2,1,0:T(8,128)(2,1)}), bf16[8,64,512]{2,1,0:T(8,128)(2,1)S(1)}, u32[]{:S(2)}, u32[]{:S(2)}) %all-to-all-start.3) | async-done | bytes 524320 | tf_op jit(solution)/shard_map/all_to_all | solution.py:28
  493.7 21.1 %psum.15 = f32[64]{0:T(128)S(1)} all-reduce(f32[64]{0:T(128)S(1)} %get-tuple-element.14), channel_id=1, replica_groups=mesh['fsdp'=16,'tp'=8] {'tp'}, use_global_device_ids=true, to_apply=%region_23.24 | all-reduce | flops 64 | bytes 512 | tf_op jit(solution)/shard_map/psum | solution.py:205
  519.6 9.3 %all-to-all-done.6 = bf16[8,64,512]{2,1,0:T(8,128)(2,1)S(1)} async-done(((bf16[8,64,512]{2,1,0:T(8,128)(2,1)}), bf16[8,64,512]{2,1,0:T(8,128)(2,1)S(1)}, u32[]{:S(2)}, u32[]{:S(2)}) %all-to-all-start.6) | async-done | bytes 524320 | tf_op jit(solution)/shard_map/all_to_all | solution.py:34
  529.7 7.9 %fusion.123 = f32[8,8,192]{2,1,0:T(8,128)S(1)} fusion(bf16[8,8,4096]{2,1,0:T(8,128)(2,1)S(1)} %convolution_convert_fusion, bf16[8,192,4096]{2,1,0:T(8,128)(2,1)} %squeeze.6), kind=kOutput, calls=%fused_computation.192 | convolution fusion | flops 100663296 | bytes 13156352 | tf_op jit(solution)/shard_map/ecd,ehd->ech/dot_general | solution.py:135
  537.7 14.4 %fusion.38 = f32[8,8,4096]{2,1,0:T(8,128)} fusion(bf16[8,192,4096]{2,1,0:T(8,128)(2,1)} %squeeze.16, bf16[8,8,4096]{2,1,0:T(8,128)(2,1)S(1)} %convolution_convert_fusion, bf16[8,192,4096]{2,1,0:T(8,128)(2,1)} %squeeze.7, f32[8,8,192]{2,1,0:T(8,128)S(1)} %fusion.123), kind=kOutput, calls=%fused_computation.47 | convolution fusion | flops 201400320 | bytes 26787840 | tf_op jit(solution)/shard_map/ech,ehd->ecd/dot_general | solution.py:138
  559.9 8.8 %all-to-all-done.7 = bf16[8,64,512]{2,1,0:T(8,128)(2,1)S(1)} async-done(((bf16[8,64,512]{2,1,0:T(8,128)(2,1)}), bf16[8,64,512]{2,1,0:T(8,128)(2,1)S(1)}, u32[]{:S(2)}, u32[]{:S(2)}) %all-to-all-start.7) | async-done | bytes 524320 | tf_op jit(solution)/shard_map/all_to_all | solution.py:28
  (107 shorter events, 55.4 us)
Async XLA Ops:
  7.2 82.6 %copy-start = (bf16[8,256,512]{2,1,0:T(8,128)(2,1)S(1)}, bf16[8,256,512]{2,1,0:T(8,128)(2,1)}, u32[]{:S(2)}) copy-start(bf16[8,256,512]{2,1,0:T(8,128)(2,1)} %param.16) | copy-start | bytes 6291460
  7.2 288.8 %all-gather.2.cloned.1.call-start = ((), (), s32[]{:S(2)}) async-start(), calls=%async_computation.8 | async-start | bytes 40108032 | tf_op jit(solution)/shard_map/all_gather | solution.py:185
  81.6 7.8 %copy-start.2 = (bf16[2,8,8192]{2,1,0:T(8,128)(2,1)S(1)}, bf16[2,8,8192]{2,1,0:T(8,128)(2,1)}, u32[]{:S(2)}) copy-start(bf16[2,8,8192]{2,1,0:T(8,128)(2,1)} %param.15) | copy-start | bytes 786436
  81.6 7.9 %copy-start.5 = (bf16[2,8,512]{2,1,0:T(8,128)(2,1)S(1)}, bf16[2,8,512]{2,1,0:T(8,128)(2,1)}, u32[]{:S(2)}) copy-start(bf16[2,8,512]{2,1,0:T(8,128)(2,1)} %param.19) | copy-start | bytes 49156
  81.6 7.9 %copy-start.7 = (s32[8]{0:T(128)S(1)}, s32[8]{0:T(128)}, u32[]{:S(2)}) copy-start(s32[8]{0:T(128)} %param.20) | copy-start | bytes 100
  81.6 8.0 %copy-start.6 = (bf16[2,8,512]{2,1,0:T(8,128)(2,1)S(1)}, bf16[2,8,512]{2,1,0:T(8,128)(2,1)}, u32[]{:S(2)}) copy-start(bf16[2,8,512]{2,1,0:T(8,128)(2,1)} %param.18) | copy-start | bytes 49156
  89.4 2.0 copy-start.8
  90.5 6.0 %copy-start.3 = (s32[2,64,8]{1,2,0:T(8,128)S(1)}, s32[2,64,8]{1,2,0:T(8,128)}, u32[]{:S(2)}) copy-start(s32[2,64,8]{1,2,0:T(8,128)} %param.21) | copy-start | bytes 12292
  91.9 8.5 %copy-start.4 = (f32[2,64,8]{1,2,0:T(8,128)S(1)}, f32[2,64,8]{1,2,0:T(8,128)}, u32[]{:S(2)}) copy-start(f32[2,64,8]{1,2,0:T(8,128)} %param.22) | copy-start | bytes 12292
  92.7 11.9 %all-to-all-start = ((bf16[8,8,1024]{2,0,1:T(8,128)(2,1)}), bf16[8,8,1024]{2,0,1:T(8,128)(2,1)S(1)}, u32[]{:S(2)}, u32[]{:S(2)}) async-start(bf16[8,8,1024]{2,0,1:T(8,128)(2,1)} %copy.83), calls=%async_computation | async-start | bytes 262144 | tf_op jit(solution)/shard_map/all_to_all | solution.py:199
  110.7 14.8 %all-to-all-start.1 = ((bf16[8,64,512]{2,1,0:T(8,128)(2,1)}), bf16[8,64,512]{2,1,0:T(8,128)(2,1)S(1)}, u32[]{:S(2)}, u32[]{:S(2)}) async-start(bf16[8,64,512]{2,1,0:T(8,128)(2,1)} %bitcast.171), calls=%async_computation.1 | async-start | bytes 1048576 | tf_op jit(solution)/shard_map/all_to_all | solution.py:28
  125.5 29.5 %all-to-all-start.4 = ((bf16[8,8,1024]{2,0,1:T(8,128)(2,1)}), bf16[8,8,1024]{2,0,1:T(8,128)(2,1)S(1)}, u32[]{:S(2)}, u32[]{:S(2)}) async-start(bf16[8,8,1024]{2,0,1:T(8,128)(2,1)} %copy.98), calls=%async_computation.4 | async-start | bytes 262144 | tf_op jit(solution)/shard_map/all_to_all | solution.py:199
  155.8 13.2 %all-to-all-start.2 = ((bf16[8,64,512]{2,1,0:T(8,128)(2,1)}), bf16[8,64,512]{2,1,0:T(8,128)(2,1)S(1)}, u32[]{:S(2)}, u32[]{:S(2)}) async-start(bf16[8,64,512]{2,1,0:T(8,128)(2,1)} %broadcast_in_dim.124), calls=%async_computation.2 | async-start | bytes 1048576 | tf_op jit(solution)/shard_map/all_to_all | solution.py:34
  169.0 306.8 %all-to-all-start.5 = ((bf16[8,64,512]{2,1,0:T(8,128)(2,1)}), bf16[8,64,512]{2,1,0:T(8,128)(2,1)S(1)}, u32[]{:S(2)}, u32[]{:S(2)}) async-start(bf16[8,64,512]{2,1,0:T(8,128)(2,1)} %bitcast.167), calls=%async_computation.5 | async-start | bytes 1048576 | tf_op jit(solution)/shard_map/all_to_all | solution.py:28
  475.8 17.7 %all-to-all-start.3 = ((bf16[8,64,512]{2,1,0:T(8,128)(2,1)}), bf16[8,64,512]{2,1,0:T(8,128)(2,1)S(1)}, u32[]{:S(2)}, u32[]{:S(2)}) async-start(bf16[8,64,512]{2,1,0:T(8,128)(2,1)} %bitcast.169), calls=%async_computation.3 | async-start | bytes 1048576 | tf_op jit(solution)/shard_map/all_to_all | solution.py:28
  515.8 13.1 %all-to-all-start.6 = ((bf16[8,64,512]{2,1,0:T(8,128)(2,1)}), bf16[8,64,512]{2,1,0:T(8,128)(2,1)S(1)}, u32[]{:S(2)}, u32[]{:S(2)}) async-start(bf16[8,64,512]{2,1,0:T(8,128)(2,1)} %broadcast_in_dim.130), calls=%async_computation.6 | async-start | bytes 1048576 | tf_op jit(solution)/shard_map/all_to_all | solution.py:34
  537.6 31.8 %copy-start.1 = (bf16[8,256,512]{2,1,0:T(8,128)(2,1)S(1)}, bf16[8,256,512]{2,1,0:T(8,128)(2,1)}, u32[]{:S(2)}) copy-start(bf16[8,256,512]{2,1,0:T(8,128)(2,1)} %param.16) | copy-start | bytes 6291460
  555.7 13.1 %all-to-all-start.7 = ((bf16[8,64,512]{2,1,0:T(8,128)(2,1)}), bf16[8,64,512]{2,1,0:T(8,128)(2,1)S(1)}, u32[]{:S(2)}, u32[]{:S(2)}) async-start(bf16[8,64,512]{2,1,0:T(8,128)(2,1)} %bitcast.165), calls=%async_computation.7 | async-start | bytes 1048576 | tf_op jit(solution)/shard_map/all_to_all | solution.py:28
Sparse Core Ops, SparseCore 0:
  89.5 206.4 all-gather.1
where the time goes:
time: 579 us; the launch traced here: 576 us
  waiting for transfers between devices  167 us (29%)
  blocking collectives  115 us (20%)
  local copies, waits for them, and re-layouts  95.3 us (16%)
  other arithmetic  90.6 us (16%)
  matrix products  61.6 us (11%)
  starting transfers between devices  31.9 us (6%)
  between operations  14.5 us (3%)
    all_gather x1, waiting for transfers between devices, local(): gathered = lax.all_gather(quantized, 'fsdp', axis=2, tiled=True)  122 us
    pmax x1, blocking collectives, local(): block_max = lax.pmax(partial_max, ('fsdp', 'tp'))  69.4 us
    squeeze x3, local copies, waits for them, and re-layouts, local_experts(): outputs = expert_rows(selected, restored[0], restored[1], restored[2])  57.9 us
    psum x2, blocking collectives, local(): squares = lax.psum(jnp.sum(values * values, axis=1), 'tp')  46.1 us
    convert_element_type x1, other arithmetic, dequantize(): (tiles * factors[..., None]).astype(jnp.bfloat16).reshape(3, WIN, count, D)  38.8 us
    reshape x1, other arithmetic, dequantize(): shard_piece.astype(jnp.float32).reshape(3, WIN, count, D // BLOCK, BLOCK)  36.6 us
    all_to_all x4, waiting for transfers between devices, sent_and_summed(): lax.all_to_all(blocks, axis, split_axis=0, concat_axis=0, tiled=True)  27.3 us
    slice x1, local copies, waits for them, and re-layouts, local_experts(): outputs = expert_rows(selected, restored[0], restored[1], restored[2])  25.3 us
  transfers between devices with their start and end apart: 9, of which 7 were waited for; matrix products, arithmetic and copies ran while one was open for 36% of the time, Pallas kernels for 0%

commit v1 on v0

--- a/solution.py
+++ b/solution.py
@@ -182,7 +182,10 @@
         .astype(jnp.bfloat16)
         .reshape(3, WIN, shard_rows, D)
     )
-    gathered = lax.all_gather(quantized, "fsdp", axis=2, tiled=True)
+    count_2 = lax.axis_size("fsdp")
+    pieces = jnp.stack([quantized for _ in range(count_2)])
+    pieces = lax.all_to_all(pieces, "fsdp", split_axis=0, concat_axis=0)
+    gathered = jnp.concatenate(pieces, axis=2)
     restored = dequantize(gathered, shard_rows, tp_count, tp_pos, scales)
     share_cols = D // tp_count
     own_start = tp_pos * share_cols

time: 579 us -> 1180 us (2.04)
  waiting for transfers between devices: 167 us -> 613 us
  local copies, waits for them, and re-layouts: 95.3 us -> 211 us
  matrix products: 61.6 us -> 98.8 us
  between operations: 14.5 us -> 1.8 us
  starting transfers between devices: 31.9 us -> 43.7 us
    all_to_all x0 -> x1, waiting for transfers between devices: none -> 579 us  [local(): pieces = lax.all_to_all(pieces, 'fsdp', split_axis=0, concat_axis=0)]
    all_gather x1 -> x0, waiting for transfers between devices: 122 us -> none  [local(): gathered = lax.all_gather(quantized, 'fsdp', axis=2, tiled=True)]
    unnamed x22 -> x65, local copies, waits for them, and re-layouts: 0.82 us -> 51.6 us
    convert_element_type x0 -> x1, local copies, waits for them, and re-layouts: none -> 50.2 us  [dequantize(): shard_piece.astype(jnp.float32).reshape(3, WIN, count, D // BLOCK, BLOCK)]
    reshape x1 -> x0, other arithmetic: 36.6 us -> none  [dequantize(): shard_piece.astype(jnp.float32).reshape(3, WIN, count, D // BLOCK, BLOCK)]
    convert_element_type x0 -> x1, other arithmetic: none -> 36.6 us  [dequantize(): shard_piece.astype(jnp.float32).reshape(3, WIN, count, D // BLOCK, BLOCK)]
    dot_general x0 -> x2, matrix products: none -> 26.5 us  [expert_rows(): jnp.einsum('ecd,ehd->ech', selected, up_rows, preferred_element_type=jnp....]
    another operation x1 -> x2, local copies, waits for them, and re-layouts: 0.01 us -> 13.6 us  [the longest x1 13.5 us: local(): pieces = jnp.stack([quantized for _ in range(count_2)])]
  transfers between devices with their start and end apart: 9 -> 9, of which waited for: 7 -> 6; matrix products, arithmetic and copies ran while one was open for 36% -> 28% of each run, Pallas kernels for 0% -> 0%
where the time goes in v1:
time: 1180 us; the launch traced here: 1170 us
  waiting for transfers between devices  613 us (52%)
  local copies, waits for them, and re-layouts  211 us (18%)
  blocking collectives  114 us (10%)
  matrix products  98.8 us (8%)
  other arithmetic  92.4 us (8%)
  starting transfers between devices  43.7 us (4%)
    all_to_all x1, waiting for transfers between devices, local(): pieces = lax.all_to_all(pieces, 'fsdp', split_axis=0, concat_axis=0)  579 us
    pmax x1, blocking collectives, local(): block_max = lax.pmax(partial_max, ('fsdp', 'tp'))  68.2 us
    squeeze x3, local copies, waits for them, and re-layouts, local_experts(): outputs = expert_rows(selected, restored[0], restored[1], restored[2])  58 us
    unnamed x65, local copies, waits for them, and re-layouts  51.6 us
    convert_element_type x1, local copies, waits for them, and re-layouts, dequantize(): shard_piece.astype(jnp.float32).reshape(3, WIN, count, D // BLOCK, BLOCK)  50.2 us
    psum x2, blocking collectives, local(): squares = lax.psum(jnp.sum(values * values, axis=1), 'tp')  45.7 us
    convert_element_type x1, other arithmetic, dequantize(): (tiles * factors[..., None]).astype(jnp.bfloat16).reshape(3, WIN, count, D)  37.9 us
    convert_element_type x1, other arithmetic, dequantize(): shard_piece.astype(jnp.float32).reshape(3, WIN, count, D // BLOCK, BLOCK)  36.6 us
  transfers between devices with their start and end apart: 9, of which 6 were waited for; matrix products, arithmetic and copies ran while one was open for 28% of the time, Pallas kernels for 0%

profile of v1, /device:TPU:0, one launch (start us, length us, event | category | flops | bytes accessed | tf_op | source)
XLA Modules:
  0.0 1174.5 jit_solution(4109676590047936161)
XLA Ops:
  35.3 68.2 %pmax.7 = f32[3,8,12,32]{3,2,1,0:T(8,128)S(1)} all-reduce(f32[3,8,12,32]{3,2,1,0:T(8,128)S(1)} %copy.91), channel_id=1, replica_groups=mesh['fsdp'=16,'tp'=8] {'fsdp','tp'}, use_global_device_ids=true, to_apply=%region_11.12 | all-reduce | flops 9216 | bytes 73728 | tf_op jit(solution)/shard_map/pmax | solution.py:175
  110.0 24.6 %psum.14 = f32[64]{0:T(128)S(1)} all-reduce(f32[64]{0:T(128)S(1)} %get-tuple-element.16), channel_id=1, replica_groups=mesh['fsdp'=16,'tp'=8] {'tp'}, use_global_device_ids=true, to_apply=%region_8.9 | all-reduce | flops 64 | bytes 512 | tf_op jit(solution)/shard_map/psum | solution.py:208
  139.1 7.4 multiply_convert_fusion.1
  148.7 13.5 %stack.31 = bf16[16,3,8,12,4096]{4,2,3,1,0:T(8,128)(2,1)} broadcast(bf16[3,8,12,4096]{3,1,2,0:T(8,128)(2,1)} %multiply_convert_fusion.1), dimensions={1,2,3,4} | broadcast | bytes 40108032 | tf_op jit(solution)/shard_map/stack | solution.py:186
  180.9 578.7 %all-to-all-done.3 = bf16[16,3,8,12,4096]{4,2,3,1,0:T(8,128)(2,1)} async-done(((bf16[16,3,8,12,4096]{4,2,3,1,0:T(8,128)(2,1)}), bf16[16,3,8,12,4096]{4,2,3,1,0:T(8,128)(2,1)}, u32[]{:S(2)}, u32[]{:S(2)}) %all-to-all-start.3) | async-done | bytes 37748768 | tf_op jit(solution)/shard_map/all_to_all | solution.py:187
  764.5 36.6 %convert_bitcast_fusion = f32[3,8,16,12,4096]{4,1,3,0,2:T(8,128)} fusion(bf16[16,3,8,12,4096]{4,2,3,1,0:T(8,128)(2,1)} %all-to-all-done.3), kind=kLoop, calls=%fused_computation | loop fusion | flops 18874368 | bytes 113246208 | tf_op jit(solution)/shard_map/convert_element_type | solution.py:74
  801.1 50.2 %copy.93 = f32[3,8,16,12,4096]{4,1,3,2,0:T(8,128)} copy(f32[3,8,16,12,4096]{4,1,3,0,2:T(8,128)} %convert_bitcast_fusion) | data formatting | bytes 150994944 | tf_op jit(solution)/shard_map/convert_element_type | solution.py:74
  851.3 49.6 %copy.125 = f32[576,8,32,128]{3,2,1,0:T(8,128)} copy(f32[576,8,32,128]{3,1,2,0:T(8,128)} %bitcast.63) | data formatting | bytes 150994944
  900.9 37.9 %multiply_convert_fusion = bf16[3,8,192,32,128]{4,3,1,2,0:T(8,128)(2,1)} fusion(f32[3,8,192,32,128]{4,3,1,2,0:T(8,128)} %bitcast.66, f32[3,8,192,32]{3,1,2,0:T(8,128)} %copy.94), kind=kLoop, calls=%fused_computation.1 | loop fusion | flops 37748736 | bytes 113836032 | tf_op jit(solution)/shard_map/convert_element_type | solution.py:75
  938.8 25.8 %fusion.125 = (bf16[1,8,192,32,128]{4,3,1,2,0:T(8,128)(2,1)}, bf16[1,8,192,32,128]{4,3,1,2,0:T(8,128)(2,1)}, bf16[1,8,192,32,128]{4,3,1,2,0:T(8,128)(2,1)}) fusion(bf16[3,8,192,32,128]{4,3,1,2,0:T(8,128)(2,1)} %multiply_convert_fusion), kind=kLoop, calls=%fused_computation.184 | loop fusion | bytes 75497472 | tf_op jit(solution)/shard_map/slice | solution.py:142
  964.5 19.3 %reshape.302 = bf16[8,192,4096]{2,0,1:T(8,128)(2,1)} reshape(bf16[1,8,192,32,128]{4,3,1,2,0:T(8,128)(2,1)} %get-tuple-element.19) | data formatting | bytes 25165824 | tf_op jit(solution)/shard_map/squeeze | solution.py:142
  983.8 19.3 %reshape.301 = bf16[8,192,4096]{2,0,1:T(8,128)(2,1)} reshape(bf16[1,8,192,32,128]{4,3,1,2,0:T(8,128)(2,1)} %get-tuple-element.20) | data formatting | bytes 25165824 | tf_op jit(solution)/shard_map/squeeze | solution.py:142
  1003.1 19.4 %reshape.303 = bf16[8,192,4096]{2,0,1:T(8,128)(2,1)} reshape(bf16[1,8,192,32,128]{4,3,1,2,0:T(8,128)(2,1)} %get-tuple-element.18) | data formatting | bytes 25165824 | tf_op jit(solution)/shard_map/squeeze | solution.py:142
  1022.5 12.9 %fusion.10 = f32[8,8,192]{2,1,0:T(8,128)S(1)} fusion(bf16[8,8,4096]{2,1,0:T(8,128)(2,1)S(1)} %copy-done.3, bf16[8,192,4096]{2,0,1:T(8,128)(2,1)} %reshape.301), kind=kOutput, calls=%fused_computation.12 | convolution fusion | flops 100663296 | bytes 13156352 | tf_op jit(solution)/shard_map/ecd,ehd->ech/dot_general | solution.py:135
  1035.4 13.4 %fusion.48 = bf16[8,8,192]{2,1,0:T(8,128)(2,1)S(1)} fusion(bf16[8,8,4096]{2,1,0:T(8,128)(2,1)S(1)} %copy-done.3, bf16[8,192,4096]{2,0,1:T(8,128)(2,1)} %reshape.302, f32[8,8,192]{2,1,0:T(8,128)S(1)} %fusion.10), kind=kOutput, calls=%fused_computation.48 | convolution fusion | flops 100737024 | bytes 13180928 | tf_op jit(solution)/shard_map/ecd,ehd->ech/dot_general | solution.py:136
  1048.8 13.3 %fusion.2 = f32[8,8,4096]{2,1,0:T(8,128)S(1)} fusion(bf16[8,8,192]{2,1,0:T(8,128)(2,1)S(1)} %fusion.48, bf16[8,192,4096]{2,0,1:T(8,128)(2,1)S(1)} %bitcast.181), kind=kOutput, calls=%fused_computation.4 | convolution fusion | flops 100663296 | bytes 13656064 | tf_op jit(solution)/shard_map/ech,ehd->ecd/dot_general | solution.py:138
  1064.6 7.2 all-to-all-start.4
  1073.2 8.9 all-to-all-done.4
  1082.3 21.2 %psum.15 = f32[64]{0:T(128)S(1)} all-reduce(f32[64]{0:T(128)S(1)} %get-tuple-element.14), channel_id=1, replica_groups=mesh['fsdp'=16,'tp'=8] {'tp'}, use_global_device_ids=true, to_apply=%region_23.24 | all-reduce | flops 64 | bytes 512 | tf_op jit(solution)/shard_map/psum | solution.py:208
  1108.0 9.5 all-to-all-done.7
  1118.4 12.9 %fusion.8 = f32[8,8,192]{2,1,0:T(8,128)S(1)} fusion(bf16[8,8,4096]{2,1,0:T(8,128)(2,1)S(1)} %convolution_convert_fusion, bf16[8,192,4096]{2,0,1:T(8,128)(2,1)} %reshape.301), kind=kOutput, calls=%fused_computation.10 | convolution fusion | flops 100663296 | bytes 13156352 | tf_op jit(solution)/shard_map/ecd,ehd->ech/dot_general | solution.py:135
  1131.3 13.1 %fusion.54 = bf16[8,8,192]{2,1,0:T(8,128)(2,1)S(1)} fusion(bf16[8,8,4096]{2,1,0:T(8,128)(2,1)S(1)} %convolution_convert_fusion, bf16[8,192,4096]{2,0,1:T(8,128)(2,1)} %reshape.302, f32[8,8,192]{2,1,0:T(8,128)S(1)} %fusion.8), kind=kOutput, calls=%fused_computation.50 | convolution fusion | flops 100737024 | bytes 13180928 | tf_op jit(solution)/shard_map/ecd,ehd->ech/dot_general | solution.py:136
  1144.5 13.4 %fusion = f32[8,8,4096]{2,1,0:T(8,128)S(1)} fusion(bf16[8,8,192]{2,1,0:T(8,128)(2,1)S(1)} %fusion.54, bf16[8,192,4096]{2,0,1:T(8,128)(2,1)S(1)} %bitcast.183), kind=kOutput, calls=%fused_computation.2 | convolution fusion | flops 100663296 | bytes 13656064 | tf_op jit(solution)/shard_map/ech,ehd->ecd/dot_general | solution.py:138
  1164.6 8.8 all-to-all-done.8
  (155 shorter events, 87.9 us)
Async XLA Ops:
  6.6 14.9 %all-to-all-start = ((bf16[8,8,1024]{2,0,1:T(8,128)(2,1)}), bf16[8,8,1024]{2,0,1:T(8,128)(2,1)S(1)}, u32[]{:S(2)}, u32[]{:S(2)}) async-start(bf16[8,8,1024]{2,0,1:T(8,128)(2,1)} %copy.86), calls=%async_computation | async-start | bytes 262144 | tf_op jit(solution)/shard_map/all_to_all | solution.py:202
  27.3 77.5 %all-to-all-start.1 = ((bf16[8,64,512]{2,1,0:T(8,128)(2,1)}), bf16[8,64,512]{2,1,0:T(8,128)(2,1)S(1)}, u32[]{:S(2)}, u32[]{:S(2)}) async-start(bf16[8,64,512]{2,1,0:T(8,128)(2,1)} %bitcast.179), calls=%async_computation.1 | async-start | bytes 1048576 | tf_op jit(solution)/shard_map/all_to_all | solution.py:28
  103.5 65.5 %copy-start.4 = (f32[3,8,12,32]{3,2,1,0:T(8,128)}, f32[3,8,12,32]{3,2,1,0:T(8,128)S(1)}, u32[]{:S(2)}) copy-start(f32[3,8,12,32]{3,2,1,0:T(8,128)S(1)} %pmax.7) | copy-start | bytes 110596
  104.8 41.6 %copy-start.12 = (f32[512]{0:T(512)}, f32[512]{0:T(512)S(1)}, u32[]{:S(2)}) copy-start(f32[512]{0:T(512)S(1)} %dynamic_slice.8) | copy-start | bytes 6148
  104.8 29.9 %all-to-all-start.5 = ((bf16[8,8,1024]{2,0,1:T(8,128)(2,1)}), bf16[8,8,1024]{2,0,1:T(8,128)(2,1)S(1)}, u32[]{:S(2)}, u32[]{:S(2)}) async-start(bf16[8,8,1024]{2,0,1:T(8,128)(2,1)} %copy.104), calls=%async_computation.5 | async-start | bytes 262144 | tf_op jit(solution)/shard_map/all_to_all | solution.py:202
  110.0 36.4 %copy-start.6 = (bf16[64,512]{1,0:T(8,128)(2,1)}, bf16[64,512]{1,0:T(8,128)(2,1)S(1)}, u32[]{:S(2)}) copy-start(bf16[64,512]{1,0:T(8,128)(2,1)S(1)} %get-tuple-element.17) | copy-start | bytes 196612
  135.6 13.1 %all-to-all-start.2 = ((bf16[8,64,512]{2,1,0:T(8,128)(2,1)}), bf16[8,64,512]{2,1,0:T(8,128)(2,1)S(1)}, u32[]{:S(2)}, u32[]{:S(2)}) async-start(bf16[8,64,512]{2,1,0:T(8,128)(2,1)} %broadcast_in_dim.124), calls=%async_computation.2 | async-start | bytes 1048576 | tf_op jit(solution)/shard_map/all_to_all | solution.py:34
  162.2 597.4 %all-to-all-start.3 = ((bf16[16,3,8,12,4096]{4,2,3,1,0:T(8,128)(2,1)}), bf16[16,3,8,12,4096]{4,2,3,1,0:T(8,128)(2,1)}, u32[]{:S(2)}, u32[]{:S(2)}) async-start(bf16[16,3,8,12,4096]{4,2,3,1,0:T(8,128)(2,1)} %stack.31), calls=%async_computation.3 | async-start | bytes 75497472 | tf_op jit(solution)/shard_map/all_to_all | solution.py:187
  759.6 305.0 %all-to-all-start.6 = ((bf16[8,64,512]{2,1,0:T(8,128)(2,1)}), bf16[8,64,512]{2,1,0:T(8,128)(2,1)}, u32[]{:S(2)}, u32[]{:S(2)}) async-start(bf16[8,64,512]{2,1,0:T(8,128)(2,1)} %bitcast.175), calls=%async_computation.6 | async-start | bytes 1048576 | tf_op jit(solution)/shard_map/all_to_all | solution.py:28
  1003.1 19.4 %copy-start.3 = (bf16[8,8,4096]{2,1,0:T(8,128)(2,1)S(1)}, bf16[8,8,4096]{2,1,0:T(8,128)(2,1)}, u32[]{:S(2)}) copy-start(bf16[8,8,4096]{2,1,0:T(8,128)(2,1)} %convolution_convert_fusion.2) | copy-start | bytes 1572868
  1022.5 26.3 %slice-start = ((s8[12582912]{0:T(1024)(128)(4,1)}), s8[4194304]{0:T(1024)(128)(4,1)S(1)}, s32[]{:S(2)}) async-start(s8[12582912]{0:T(1024)(128)(4,1)} %bitcast.180), calls=%async_computation.9 | async-start | bytes 8388608
  1022.5 26.3 %slice-start.1 = ((s8[12582912]{0:T(1024)(128)(4,1)}), s8[4194304]{0:T(1024)(128)(4,1)S(1)}, s32[]{:S(2)}) async-start(s8[12582912]{0:T(1024)(128)(4,1)} %bitcast.180), calls=%async_computation.10 | async-start | bytes 8388608
  1048.8 23.0 %copy-start.11 = (s32[64,8]{0,1:T(8,128)S(1)}, s32[64,8]{0,1:T(8,128)}, u32[]{:S(2)}) copy-start(s32[64,8]{0,1:T(8,128)} %copy-done.10) | copy-start | bytes 6148
  1062.1 20.1 %copy-start.7 = (bf16[64,512]{1,0:T(8,128)(2,1)S(1)}, bf16[64,512]{1,0:T(8,128)(2,1)}, u32[]{:S(2)}) copy-start(bf16[64,512]{1,0:T(8,128)(2,1)} %copy-done.6) | copy-start | bytes 196612
  1062.2 41.4 %copy-start.13 = (f32[512]{0:T(512)S(1)}, f32[512]{0:T(512)}, u32[]{:S(2)}) copy-start(f32[512]{0:T(512)} %copy-done.12) | copy-start | bytes 6148
  1062.2 45.8 %copy-start.15 = (f32[8,64]{1,0:T(8,128)S(1)}, f32[8,64]{1,0:T(8,128)}, u32[]{:S(2)}) copy-start(f32[8,64]{1,0:T(8,128)} %get-tuple-element.34) | copy-start | bytes 6148
  1062.2 45.8 %copy-start.22 = (f32[64]{0:T(128)S(1)}, f32[64]{0:T(128)}, u32[]{:S(2)}) copy-start(f32[64]{0:T(128)} %get-tuple-element.10) | copy-start | bytes 772
  1064.6 17.5 %all-to-all-start.4 = ((bf16[8,64,512]{2,1,0:T(8,128)(2,1)}), bf16[8,64,512]{2,1,0:T(8,128)(2,1)S(1)}, u32[]{:S(2)}, u32[]{:S(2)}) async-start(bf16[8,64,512]{2,1,0:T(8,128)(2,1)} %bitcast.177), calls=%async_computation.4 | async-start | bytes 1048576 | tf_op jit(solution)/shard_map/all_to_all | solution.py:28
  1104.5 13.1 %all-to-all-start.7 = ((bf16[8,64,512]{2,1,0:T(8,128)(2,1)}), bf16[8,64,512]{2,1,0:T(8,128)(2,1)S(1)}, u32[]{:S(2)}, u32[]{:S(2)}) async-start(bf16[8,64,512]{2,1,0:T(8,128)(2,1)} %broadcast_in_dim.130), calls=%async_computation.7 | async-start | bytes 1048576 | tf_op jit(solution)/shard_map/all_to_all | solution.py:34
  1118.4 26.1 %slice-start.3 = ((s8[12582912]{0:T(1024)(128)(4,1)}), s8[4194304]{0:T(1024)(128)(4,1)S(1)}, s32[]{:S(2)}) async-start(s8[12582912]{0:T(1024)(128)(4,1)} %bitcast.182), calls=%async_computation.12 | async-start | bytes 8388608
  1118.4 26.1 %slice-start.4 = ((s8[12582912]{0:T(1024)(128)(4,1)}), s8[4194304]{0:T(1024)(128)(4,1)S(1)}, s32[]{:S(2)}) async-start(s8[12582912]{0:T(1024)(128)(4,1)} %bitcast.182), calls=%async_computation.13 | async-start | bytes 8388608
  1144.5 19.3 %copy-start.5 = (f32[3,8,12,32]{3,2,1,0:T(8,128)S(1)}, f32[3,8,12,32]{3,2,1,0:T(8,128)}, u32[]{:S(2)}) copy-start(f32[3,8,12,32]{3,2,1,0:T(8,128)} %copy-done.4) | copy-start | bytes 110596
  1144.5 29.6 %copy-start.1 = (bf16[8,256,512]{2,1,0:T(8,128)(2,1)S(1)}, bf16[8,256,512]{2,1,0:T(8,128)(2,1)}, u32[]{:S(2)}) copy-start(bf16[8,256,512]{2,1,0:T(8,128)(2,1)} %param.16) | copy-start | bytes 6291460
  1160.3 13.1 %all-to-all-start.8 = ((bf16[8,64,512]{2,1,0:T(8,128)(2,1)}), bf16[8,64,512]{2,1,0:T(8,128)(2,1)S(1)}, u32[]{:S(2)}, u32[]{:S(2)}) async-start(bf16[8,64,512]{2,1,0:T(8,128)(2,1)} %bitcast.173), calls=%async_computation.8 | async-start | bytes 1048576 | tf_op jit(solution)/shard_map/all_to_all | solution.py:28
  (15 other events, 136.9 us)
